TPU v7x, 32 devices: a whole 2x2x4 slice. The times are simulated.
32 devices in a mesh: fsdp: 8 (over y, x, core), tensor: 4 (over z).
Axes of the slice: x: 2, y: 2, z: 4, core: 2. Of those that a mesh axis runs over, the one named last changes fastest.
Arguments:
- hidden_t: bfloat16 [28672, 512], P('fsdp', 'tensor'), may hold values from -6 to 6
- down_weight: bfloat16 [28672, 4096], P('fsdp', 'tensor'), may hold values from -0.03125 to 0.03125
- probe: bfloat16 [28672, 4096], P('fsdp', 'tensor'), may hold values from -5 to 5
- grad_moment: bfloat16 [28672, 4096], P('fsdp', 'tensor'), may hold values from -0.0059814453 to 0.0059814453
- curv_moment: bfloat16 [28672, 4096], P('fsdp', 'tensor'), may hold values from 0.0099487305 to 0.099609375
- target: bfloat16 [512, 4096], P('fsdp', 'tensor'), may hold values from -6 to 6
Outputs:
- new_grad_moment: bfloat16 [28672, 4096], P('fsdp', 'tensor')
- new_curv_moment: bfloat16 [28672, 4096], P('fsdp', 'tensor')
- update: bfloat16 [28672, 4096], P('fsdp', 'tensor')
All inputs are finite; a program needn't handle non-finite values.
Results may differ from a plain program's by a relative error of at most 0.0056.
Values may be sent and summed in bfloat16 or wider, within the bound.
A program may use at most 192 MiB of HBM per device.

v0:
```python
import jax
import jax.numpy as jnp
from jax import lax
from jax.sharding import PartitionSpec as P

BETA_ONE = 0.965
BETA_TWO = 0.99
RHO_SCALE = 0.02
EPS_FLOOR = 0.0005


def cotangents(summed, target_rows, col_width, token_count):
    adjoint = ((summed[:, :col_width] - target_rows.astype(jnp.float32)) / token_count).astype(
        jnp.bfloat16
    )
    tangent_adjoint = (summed[:, col_width:] / token_count).astype(jnp.bfloat16)
    return jnp.concatenate([adjoint, tangent_adjoint], axis=1)


def shards(hidden_t, down_weight, probe, grad_moment, curv_moment, target):
    gathered = lax.all_gather(hidden_t, "tensor", axis=1, tiled=True)
    col_width = down_weight.shape[1]
    token_count = gathered.shape[1]
    paired = jnp.concatenate([down_weight, probe], axis=1)
    partial_out = lax.dot_general(
        gathered, paired, (((0,), (0,)), ((), ())), preferred_element_type=jnp.float32
    )
    totals = lax.psum(partial_out, "fsdp")
    target_all = lax.all_gather(target, "fsdp", axis=0, tiled=True)
    stacked = cotangents(totals, target_all, col_width, token_count)
    products = jnp.dot(gathered, stacked, preferred_element_type=jnp.float32)
    gradient = products[:, :col_width]
    hess_probe = products[:, col_width:]
    estimate = probe.astype(jnp.float32) * hess_probe
    moment_next = BETA_ONE * grad_moment.astype(jnp.float32) + (1.0 - BETA_ONE) * gradient
    curv_next = BETA_TWO * curv_moment.astype(jnp.float32) + (1.0 - BETA_TWO) * estimate
    raw_ratio = moment_next / jnp.maximum(RHO_SCALE * curv_next, EPS_FLOOR)
    update = jnp.clip(raw_ratio, -1.0, 1.0)
    return (
        moment_next.astype(jnp.bfloat16),
        curv_next.astype(jnp.bfloat16),
        update.astype(jnp.bfloat16),
    )


def solution(mesh):
    in_specs = (
        P("fsdp", "tensor"),
        P("fsdp", "tensor"),
        P("fsdp", "tensor"),
        P("fsdp", "tensor"),
        P("fsdp", "tensor"),
        P("fsdp", "tensor"),
    )
    out_specs = (P("fsdp", "tensor"), P("fsdp", "tensor"), P("fsdp", "tensor"))
    return jax.shard_map(shards, mesh=mesh, in_specs=in_specs, out_specs=out_specs, check_vma=False)
```

profile of v0, /device:TPU:0, one launch (start us, length us, event | category | flops | bytes accessed | tf_op | source)
XLA Modules:
  0.0 273.3 jit_solution(6230435863053550682)
XLA Ops:
  7.2 0.0 all-gather.3.cloned.1.call-start
  7.2 0.7 all-gather.3.cloned.1.call-update
  7.9 0.0 all-gather.5.cloned.1.call-start
  7.9 0.7 all-gather.5.cloned.1.call-update
  8.6 0.0 all-reduce.2.cloned.1.call-start
  8.7 75.6 %all-gather.3.cloned.1.call-done = bf16[3584,512]{1,0:T(8,128)(2,1)} async-done(((bf16[3584,128]{1,0:T(8,128)(2,1)}), bf16[3584,512]{1,0:T(8,128)(2,1)}) %all-gather.3.cloned.1.call-update) | async-done | bytes 3670032 | tf_op jit(solution)/shard_map/all_gather | solution.py:21
  84.3 16.0 %fusion.8 = f32[512,2048]{0,1:T(8,128)} fusion(bf16[3584,512]{1,0:T(8,128)(2,1)} %all-gather.3.cloned.1.call-done, bf16[3584,1024]{1,0:T(8,128)(2,1)} %param.8, bf16[3584,1024]{1,0:T(8,128)(2,1)} %param.7), kind=kOutput, calls=%fused_computation.12 | convolution fusion | flops 7545552896 | bytes 22544384 | tf_op jit(solution)/shard_map/dot_general | solution.py:25
  100.3 0.0 all-reduce.2.cloned.1.call-update
  100.3 10.2 %copy.19 = bf16[3584,1024]{0,1:T(8,128)(2,1)} copy(bf16[3584,1024]{1,0:T(8,128)(2,1)} %param.8) | data formatting | bytes 14680064 | tf_op args[2]
  110.6 10.2 %copy.16 = bf16[3584,1024]{0,1:T(8,128)(2,1)} copy(bf16[3584,1024]{1,0:T(8,128)(2,1)} %param.9) | data formatting | bytes 14680064 | tf_op args[3]
  120.7 10.0 %copy.18 = bf16[3584,1024]{0,1:T(8,128)(2,1)} copy(bf16[3584,1024]{1,0:T(8,128)(2,1)} %param.10) | data formatting | bytes 14680064 | tf_op args[4]
  130.8 0.0 all-gather.5.cloned.1.call-done
  130.8 1.5 copy.17
  132.3 59.9 %all-reduce.2.cloned.1.call-done = f32[512,2048]{0,1:T(8,128)} async-done(((f32[512,2048]{0,1:T(8,128)}), f32[512,2048]{0,1:T(8,128)}) %all-reduce.2.cloned.1.call-update) | async-done | bytes 4194320 | tf_op jit(solution)/shard_map/psum | solution.py:28
  192.2 0.0 slice-start
  192.2 3.0 %fusion.14 = (bf16[512,1024]{0,1:T(8,128)(2,1)S(1)}, bf16[512,1024]{0,1:T(8,128)(2,1)S(1)}) fusion(f32[512,2048]{0,1:T(8,128)} %all-reduce.2.cloned.1.call-done, bf16[512,1024]{0,1:T(8,128)(2,1)S(1)} %copy.17), kind=kLoop, calls=%fused_computation.18 | loop fusion | flops 3145728 | bytes 7340032 | tf_op jit(solution)/shard_map/convert_element_type | solution.py:13
  195.2 0.0 slice-start.1
  195.3 16.8 %convolution_bitcast_fusion = f32[3584,2048]{0,1:T(8,128)} fusion(bf16[3584,512]{1,0:T(8,128)(2,1)} %all-gather.3.cloned.1.call-done, bf16[512,1024]{0,1:T(8,128)(2,1)S(1)} %get-tuple-element.13, bf16[512,1024]{0,1:T(8,128)(2,1)S(1)} %get-tuple-element.12), kind=kOutput, calls=%fused_computation | convolution fusion | flops 7520387072 | bytes 35127296 | tf_op jit(solution)/shard_map/dot_general | solution.py:31
  212.1 0.0 slice-done
  212.1 0.0 slice-done.1
  212.1 23.6 %clamp_convert_fusion = (bf16[3584,1024]{0,1:T(8,128)(2,1)}, bf16[3584,1024]{0,1:T(8,128)(2,1)}, bf16[3584,1024]{0,1:T(8,128)(2,1)}) fusion(f32[3584,2048]{0,1:T(8,128)} %convolution_bitcast_fusion, bf16[3584,1024]{0,1:T(8,128)(2,1)} %copy.16, bf16[3584,1024]{0,1:T(8,128)(2,1)S(1)} %bitcast.7, bf16[3584,1024]{0,1:T(8,128)(2,1)} %copy.18), kind=kLoop, calls=%fused_computation.10 | loop fusion | flops 62390272 | bytes 73400320 | tf_op jit(solution)/shard_map/convert_element_type | solution.py:42
  235.6 10.4 %copy.20 = bf16[3584,1024]{1,0:T(8,128)(2,1)} copy(bf16[3584,1024]{0,1:T(8,128)(2,1)} %get-tuple-element.11) | data formatting | bytes 14680064
  246.0 10.4 %copy.21 = bf16[3584,1024]{1,0:T(8,128)(2,1)} copy(bf16[3584,1024]{0,1:T(8,128)(2,1)} %get-tuple-element.10) | data formatting | bytes 14680064
  256.4 10.4 %copy.22 = bf16[3584,1024]{1,0:T(8,128)(2,1)} copy(bf16[3584,1024]{0,1:T(8,128)(2,1)} %get-tuple-element.9) | data formatting | bytes 14680064
  (1 shorter events, 0.0 us)
Async XLA Ops:
  7.2 77.1 %all-gather.3.cloned.1.call-start = ((), (), s32[]{:S(2)}) async-start(), calls=%async_computation | async-start | bytes 4587520 | tf_op jit(solution)/shard_map/all_gather | solution.py:21
  7.9 122.9 %all-gather.5.cloned.1.call-start = ((), (), s32[]{:S(2)}) async-start(), calls=%async_computation.2 | async-start | bytes 1179648 | tf_op jit(solution)/shard_map/all_gather | solution.py:29
  8.6 183.6 %all-reduce.2.cloned.1.call-start = ((), (), s32[]{:S(2)}) async-start(), calls=%async_computation.1 | async-start | bytes 8388608 | tf_op jit(solution)/shard_map/psum | solution.py:28
  192.2 19.9 %slice-start = ((s8[7340032]{0:T(1024)(128)(4,1)}), s8[4194304]{0:T(1024)(128)(4,1)S(1)}, s32[]{:S(2)}) async-start(s8[7340032]{0:T(1024)(128)(4,1)} %bitcast.6), calls=%async_computation.3 | async-start | bytes 8388608
  195.2 16.8 %slice-start.1 = ((s8[7340032]{0:T(1024)(128)(4,1)}), s8[3145728]{0:T(1024)(128)(4,1)S(1)}, s32[]{:S(2)}) async-start(s8[7340032]{0:T(1024)(128)(4,1)} %bitcast.6), calls=%async_computation.4 | async-start | bytes 6291456
Sparse Core Ops, SparseCore 0:
  9.6 74.6 all-gather.2
  86.2 21.6 all-gather.4
  111.2 80.9 all-reduce.1
where the time goes:
time: 275 us; the launch traced here: 273 us
  waiting for transfers between devices  137 us (50%)
  local copies, waits for them, and re-layouts  63.2 us (23%)
  matrix products  32.8 us (12%)
  other arithmetic  26.6 us (10%)
  between operations  13.8 us (5%)
    all_gather x1, waiting for transfers between devices, shards(): gathered = lax.all_gather(hidden_t, 'tensor', axis=1, tiled=True)  75.6 us
    unnamed x10, local copies, waits for them, and re-layouts  61.7 us
    psum x1, waiting for transfers between devices, shards(): totals = lax.psum(partial_out, 'fsdp')  59.9 us
    convert_element_type x1, other arithmetic, shards(): update.astype(jnp.bfloat16)  23.6 us
    dot_general x1, matrix products, shards(): products = jnp.dot(gathered, stacked, preferred_element_type=jnp.float32)  16.8 us
    dot_general x1, matrix products, shards(): lax.dot_general(gathered, paired, (((0,), (0,)), ((), ())), preferred_ele...  16 us
  transfers between devices with their start and end apart: 3, of which 2 were waited for; matrix products, arithmetic and copies ran while one was open for 18% of the time, Pallas kernels for 0%

commit v1 on v0

v1 whole, which is shorter than its diff:
```python
import functools

import jax
import jax.numpy as jnp
from jax import lax
from jax.experimental import pallas as pl
from jax.experimental.pallas import tpu as pltpu
from jax.sharding import PartitionSpec as P

BETA_ONE = 0.965
BETA_TWO = 0.99
RHO_SCALE = 0.02
EPS_FLOOR = 0.0005
MESH = pl.DeviceIdType.MESH
MIB = 1 << 20


def cotangents(summed, target_rows, col_width, token_count):
    adjoint = ((summed[:, :col_width] - target_rows.astype(jnp.float32)) / token_count).astype(
        jnp.bfloat16
    )
    tangent_adjoint = (summed[:, col_width:] / token_count).astype(jnp.bfloat16)
    return jnp.concatenate([adjoint, tangent_adjoint], axis=1)


def moments(products, probe, grad_moment, curv_moment):
    col_width = probe.shape[1]
    gradient = products[:, :col_width]
    hess_probe = products[:, col_width:]
    estimate = probe.astype(jnp.float32) * hess_probe
    moment_next = BETA_ONE * grad_moment.astype(jnp.float32) + (1.0 - BETA_ONE) * gradient
    curv_next = BETA_TWO * curv_moment.astype(jnp.float32) + (1.0 - BETA_TWO) * estimate
    raw_ratio = moment_next / jnp.maximum(RHO_SCALE * curv_next, EPS_FLOOR)
    update = jnp.clip(raw_ratio, -1.0, 1.0)
    return (
        moment_next.astype(jnp.bfloat16),
        curv_next.astype(jnp.bfloat16),
        update.astype(jnp.bfloat16),
    )


def plain_shards(hidden_t, down_weight, probe, grad_moment, curv_moment, target):
    gathered = lax.all_gather(hidden_t, "tensor", axis=1, tiled=True)
    col_width = down_weight.shape[1]
    token_count = gathered.shape[1]
    paired = jnp.concatenate([down_weight, probe], axis=1)
    partial_out = lax.dot_general(
        gathered, paired, (((0,), (0,)), ((), ())), preferred_element_type=jnp.float32
    )
    totals = lax.psum(partial_out, "fsdp")
    target_all = lax.all_gather(target, "fsdp", axis=0, tiled=True)
    stacked = cotangents(totals, target_all, col_width, token_count)
    products = jnp.dot(gathered, stacked, preferred_element_type=jnp.float32)
    return moments(products, probe, grad_moment, curv_moment)


def arrival_order(n_t):
    table = []
    for z in range(n_t):
        near_right = z < n_t // 2
        table.append(
            sorted(range(n_t), key=lambda b: (abs(b - z), (b < z) == near_right))
        )
    return table


def pick(values, index):
    result = jnp.int32(values[0])
    for i in range(1, len(values)):
        result = jnp.where(index == i, jnp.int32(values[i]), result)
    return result


def cotangent_kernel(
    n_f, n_t, n_c,
    hid_in, w_in, probe_in, target_in,
    gath, stk,
    wbuf, acc, part, rsbuf, tgt,
    hid_sem, w_sem, p_sem,
    left_send, right_send, gath_recv,
    rs_send, rs_recv, ag_send, ag_recv, tgt_send, tgt_recv,
):
    f = lax.axis_index("fsdp")
    z = lax.axis_index("tensor")
    rows, block_tokens = hid_in.shape
    cols = w_in.shape[1]
    chunk = rows // n_c
    piece = block_tokens // n_f
    tokens = block_tokens * n_t
    order = arrival_order(n_t)

    def cut(c):
        return pl.ds(pl.multiple_of(c * chunk, chunk), chunk)

    def span(j):
        return pl.ds(pl.multiple_of(j * piece, piece), piece)

    def hid_load(c):
        return pltpu.make_async_copy(
            hid_in.at[cut(c)], gath.at[z, cut(c)], hid_sem.at[c]
        )

    def w_load(c):
        return pltpu.make_async_copy(
            w_in.at[cut(c)], wbuf.at[cut(c), pl.ds(0, cols)], w_sem.at[c]
        )

    def p_load(c):
        return pltpu.make_async_copy(
            probe_in.at[cut(c)], wbuf.at[cut(c), pl.ds(cols, cols)], p_sem.at[c]
        )

    def pass_on(src, b, c, side):
        sems = left_send if side < 0 else right_send
        return pltpu.make_async_remote_copy(
            src_ref=src.at[cut(c)],
            dst_ref=gath.at[b, cut(c)],
            send_sem=sems.at[b, c],
            recv_sem=gath_recv.at[b, c],
            device_id=(f, z + side),
            device_id_type=MESH,
        )

    def rs_copy(b, peer, slot):
        return pltpu.make_async_remote_copy(
            src_ref=part.at[b, span(peer)],
            dst_ref=rsbuf.at[b, slot],
            send_sem=rs_send.at[b, peer],
            recv_sem=rs_recv.at[b, slot],
            device_id=(peer, z),
            device_id_type=MESH,
        )

    def ag_copy(b, peer, slot):
        return pltpu.make_async_remote_copy(
            src_ref=stk.at[b, span(slot)],
            dst_ref=stk.at[b, span(slot)],
            send_sem=ag_send.at[b, peer],
            recv_sem=ag_recv.at[b, slot],
            device_id=(peer, z),
            device_id_type=MESH,
        )

    def tgt_copies(k):
        index = f * n_t + k
        b, owner = index // n_f, index % n_f
        local = pltpu.make_async_copy(
            target_in.at[span(k)], tgt.at[b], tgt_recv.at[b]
        )
        remote = pltpu.make_async_remote_copy(
            src_ref=target_in.at[span(k)],
            dst_ref=tgt.at[b],
            send_sem=tgt_send.at[k],
            recv_sem=tgt_recv.at[b],
            device_id=(owner, z),
            device_id_type=MESH,
        )
        return owner, local, remote

    for c in range(n_c):
        hid_load(c).start()
        w_load(c).start()
        p_load(c).start()

    barrier = pltpu.get_barrier_semaphore()
    for d in range(1, n_f):
        pl.semaphore_signal(
            barrier, inc=1, device_id=((f + d) % n_f, z), device_id_type=MESH
        )

    @pl.when(z > 0)
    def _():
        pl.semaphore_signal(barrier, inc=1, device_id=(f, z - 1), device_id_type=MESH)

    @pl.when(z < n_t - 1)
    def _():
        pl.semaphore_signal(barrier, inc=1, device_id=(f, z + 1), device_id_type=MESH)

    near = jnp.where(z > 0, 1, 0) + jnp.where(z < n_t - 1, 1, 0)
    pl.semaphore_wait(barrier, n_f - 1 + near)

    @pl.when(z > 0)
    def _():
        for c in range(n_c):
            pass_on(hid_in, z, c, -1).start()

    @pl.when(z < n_t - 1)
    def _():
        for c in range(n_c):
            pass_on(hid_in, z, c, 1).start()

    for k in range(n_t):
        owner, local, remote = tgt_copies(k)
        pl.when(owner == f)(local.start)
        pl.when(owner != f)(remote.start)

    def finish(b):
        mine = part.at[b, span(f)]
        pltpu.make_async_copy(tgt.at[b], tgt.at[b], tgt_recv.at[b]).wait()
        for d in range(1, n_f):
            source = (f + n_f - d) % n_f
            rs_copy(b, source, source).wait_recv()
        total = mine[...].astype(jnp.float32)
        for d in range(1, n_f):
            total += rsbuf[b, (f + d) % n_f].astype(jnp.float32)
        stk[b, span(f)] = cotangents(total, tgt[b], cols, tokens)
        for d in range(1, n_f):
            ag_copy(b, (f + d) % n_f, f).start()

    for s in range(n_t):
        b = pick([order[i][s] for i in range(n_t)], z)

        def step(c, carry, s=s, b=b):
            if s == 0:
                hid_load(c).wait()
                w_load(c).wait()
                p_load(c).wait()
            else:
                pltpu.make_async_copy(
                    gath.at[b, cut(c)], gath.at[b, cut(c)], gath_recv.at[b, c]
                ).wait()

                @pl.when((b > z) & (z > 0))
                def _():
                    pass_on(gath.at[b], b, c, -1).start()

                @pl.when((b < z) & (z < n_t - 1))
                def _():
                    pass_on(gath.at[b], b, c, 1).start()

            for half in range(2):
                width = pl.ds(half * cols, cols)
                term = lax.dot_general(
                    gath[b, cut(c)],
                    wbuf[cut(c), width],
                    (((0,), (0,)), ((), ())),
                    preferred_element_type=jnp.float32,
                )
                acc[:, width] += term
            return carry

        acc[...] = jnp.zeros_like(acc)
        middle = n_c // 2
        lax.fori_loop(0, middle, step, 0)
        if s > 0:
            finish(pick([order[i][s - 1] for i in range(n_t)], z))
        lax.fori_loop(middle, n_c, step, 0)
        part[b] = acc[...].astype(jnp.bfloat16)
        for d in range(1, n_f):
            rs_copy(b, (f + d) % n_f, f).start()
    finish(pick([order[i][n_t - 1] for i in range(n_t)], z))

    def drain(b, carry):
        for d in range(1, n_f):
            source = (f + n_f - d) % n_f
            ag_copy(b, source, source).wait_recv()
            peer = (f + d) % n_f
            rs_copy(b, peer, f).wait_send()
            ag_copy(b, peer, f).wait_send()

        @pl.when((b >= z) & (z > 0))
        def _():
            for c in range(n_c):
                pass_on(hid_in, b, c, -1).wait_send()

        @pl.when((b <= z) & (z < n_t - 1))
        def _():
            for c in range(n_c):
                pass_on(hid_in, b, c, 1).wait_send()

        return carry

    lax.fori_loop(0, n_t, drain, 0)
    for k in range(n_t):
        owner, local, remote = tgt_copies(k)
        pl.when(owner != f)(remote.wait_send)


def moment_kernel(gath, stk, probe, grad_moment, curv_moment, new_grad, new_curv, update):
    n_t = gath.shape[0]
    hidden = jnp.concatenate([gath[b] for b in range(n_t)], axis=1)
    stacked = jnp.concatenate([stk[b] for b in range(n_t)], axis=0)
    products = jnp.dot(hidden, stacked, preferred_element_type=jnp.float32)
    new_grad[...], new_curv[...], update[...] = moments(
        products, probe[...], grad_moment[...], curv_moment[...]
    )


def kernel_shards(n_f, n_t, n_c, tile, hidden_t, down_weight, probe, grad_moment, curv_moment, target):
    rows, block_tokens = hidden_t.shape
    cols = down_weight.shape[1]
    piece = block_tokens // n_f
    bf16 = jnp.bfloat16
    dma = pltpu.SemaphoreType.DMA
    whole_vmem = pl.BlockSpec(memory_space=pltpu.VMEM)
    gath, stk = pl.pallas_call(
        functools.partial(cotangent_kernel, n_f, n_t, n_c),
        out_shape=(
            jax.ShapeDtypeStruct((n_t, rows, block_tokens), bf16),
            jax.ShapeDtypeStruct((n_t, block_tokens, 2 * cols), bf16),
        ),
        in_specs=[pl.BlockSpec(memory_space=pl.ANY)] * 4,
        out_specs=(whole_vmem, whole_vmem),
        scratch_shapes=[
            pltpu.VMEM((rows, 2 * cols), bf16),
            pltpu.VMEM((block_tokens, 2 * cols), jnp.float32),
            pltpu.VMEM((n_t, block_tokens, 2 * cols), bf16),
            pltpu.VMEM((n_t, n_f, piece, 2 * cols), bf16),
            pltpu.VMEM((n_t, piece, cols), bf16),
            dma((n_c,)), dma((n_c,)), dma((n_c,)),
            dma((n_t, n_c)), dma((n_t, n_c)), dma((n_t, n_c)),
            dma((n_t, n_f)), dma((n_t, n_f)), dma((n_t, n_f)), dma((n_t, n_f)),
            dma((n_t,)), dma((n_t,)),
        ],
        compiler_params=pltpu.CompilerParams(
            collective_id=0, has_side_effects=True, vmem_limit_bytes=44 * MIB
        ),
        name="cotangents",
    )(hidden_t, down_weight, probe, target)

    strip = pl.BlockSpec((tile, cols), lambda i: (i, 0))
    return pl.pallas_call(
        moment_kernel,
        grid=(rows // tile,),
        out_shape=(jax.ShapeDtypeStruct((rows, cols), bf16),) * 3,
        in_specs=[
            pl.BlockSpec((n_t, tile, block_tokens), lambda i: (0, i, 0)),
            pl.BlockSpec((n_t, block_tokens, 2 * cols), lambda i: (0, 0, 0)),
            strip, strip, strip,
        ],
        out_specs=(strip, strip, strip),
        compiler_params=pltpu.CompilerParams(vmem_limit_bytes=40 * MIB),
        name="moments",
    )(gath, stk, probe, grad_moment, curv_moment)


def solution(mesh):
    n_f, n_t = mesh.shape["fsdp"], mesh.shape["tensor"]

    def shards(hidden_t, down_weight, probe, grad_moment, curv_moment, target):
        rows, block_tokens = hidden_t.shape
        cols = down_weight.shape[1]
        n_c, tile = 7, 256
        fits = (
            n_f > 1 and n_t > 1
            and block_tokens % 128 == 0 and cols % 128 == 0
            and block_tokens % (16 * n_f) == 0
            and rows % (n_c * 128) == 0 and rows % tile == 0
        )
        args = (hidden_t, down_weight, probe, grad_moment, curv_moment, target)
        if not fits:
            return plain_shards(*args)
        return kernel_shards(n_f, n_t, n_c, tile, *args)

    spec = P("fsdp", "tensor")
    return jax.shard_map(
        shards, mesh=mesh, in_specs=(spec,) * 6, out_specs=(spec,) * 3, check_vma=False
    )
```

time: 275 us -> 107 us (0.39)
  waiting for transfers between devices: 137 us -> 0 us
  Pallas kernels: 0 us -> 103 us
  local copies, waits for them, and re-layouts: 63.2 us -> 2.45 us
  matrix products: 32.8 us -> 0 us
  other arithmetic: 26.6 us -> 0 us
  between operations: 13.8 us -> 0.66 us
    pallas_call x0 -> x2, Pallas kernels: none -> 103 us  [the longest x1 82.6 us: kernel_shards(): pl.pallas_call(functools.partial(cotangent_kernel, n_f, n_t, n_c), out_sh...]
    all_gather x2 -> x0, waiting for transfers between devices: 75.6 us -> none  [the longest x1 75.6 us: shards(): gathered = lax.all_gather(hidden_t, 'tensor', axis=1, tiled=True)]
    psum x1 -> x0, waiting for transfers between devices: 59.9 us -> none  [shards(): totals = lax.psum(partial_out, 'fsdp')]
    unnamed x10 -> x6, local copies, waits for them, and re-layouts: 61.7 us -> 2.45 us
    dot_general x2 -> x0, matrix products: 32.8 us -> none  [the longest x1 16.8 us: shards(): products = jnp.dot(gathered, stacked, preferred_element_type=jnp.float32)]
    convert_element_type x2 -> x0, other arithmetic: 26.6 us -> none  [the longest x1 23.6 us: shards(): update.astype(jnp.bfloat16)]
  transfers between devices with their start and end apart: 3 -> 0, of which waited for: 2 -> 0; matrix products, arithmetic and copies ran while one was open for 18% -> 0% of each run, Pallas kernels for 0% -> 0%
where the time goes in v1:
time: 107 us; the launch traced here: 106 us
  Pallas kernels  103 us (96%)
  local copies, waits for them, and re-layouts  2.45 us (2%)
    pallas_call x1, Pallas kernels, kernel_shards(): pl.pallas_call(functools.partial(cotangent_kernel, n_f, n_t, n_c), out_sh...  82.6 us
    pallas_call x1, Pallas kernels, kernel_shards(): pl.pallas_call(moment_kernel, grid=(rows // tile,), out_shape=(jax.ShapeD...  20.3 us
    unnamed x6, local copies, waits for them, and re-layouts  2.45 us

profile of v1, /device:TPU:0, one launch (start us, length us, event | category | flops | bytes accessed | tf_op | source)
XLA Modules:
  0.0 106.0 jit_solution(11369954737012967742)
XLA Ops:
  0.6 0.0 copy-start
  0.6 0.0 copy-start.1
  0.7 1.3 %copy-done.1 = bf16[3584,128]{1,0:T(8,128)(2,1)S(1)} copy-done((bf16[3584,128]{1,0:T(8,128)(2,1)S(1)}, bf16[3584,128]{1,0:T(8,128)(2,1)}, u32[]{:S(2)}) %copy-start.1) | copy-done | bytes 917528
  2.0 0.0 copy-start.2
  2.0 1.1 %copy-done.2 = bf16[64,1024]{1,0:T(8,128)(2,1)S(1)} copy-done((bf16[64,1024]{1,0:T(8,128)(2,1)S(1)}, bf16[64,1024]{1,0:T(8,128)(2,1)}, u32[]{:S(2)}) %copy-start.2) | copy-done | bytes 131096
  3.1 82.6 %cotangents.1 = (bf16[4,3584,128]{2,1,0:T(8,128)(2,1)S(1)}, bf16[4,128,2048]{2,1,0:T(8,128)(2,1)S(1)}) custom-call(bf16[3584,128]{1,0:T(8,128)(2,1)S(1)} %copy-done.1, bf16[3584,1024]{1,0:T(8,128)(2,1)} %w_in.1, bf16[3584,1024]{1,0:T(8,128)(2,1)} %probe.1, bf16[64,1024]{1,0:T(8,128)(2,1)S(1)} %copy-done.2), custom_call_target="tpu_custom_call" | custom-call | tf_op jit(solution)/shard_map/cotangents/pallas_call | solution.py:296
  85.7 0.0 copy-done
  85.7 20.3 %moments.1 = (bf16[3584,1024]{1,0:T(8,128)(2,1)}, bf16[3584,1024]{1,0:T(8,128)(2,1)}, bf16[3584,1024]{1,0:T(8,128)(2,1)}) custom-call(bf16[4,3584,128]{2,1,0:T(8,128)(2,1)S(1)} %get-tuple-element.5.gath, bf16[4,128,2048]{2,1,0:T(8,128)(2,1)S(1)} %get-tuple-element.6.stk, bf16[3584,1024]{1,0:T(8,128)(2,1)S(1)} %copy-done, bf16[3584,1024]{1,0:T(8,128)(2,1)} %grad_moment.1, ...), custom_call_target="tpu_custom_call" | custom-call | tf_op jit(solution)/shard_map/moments/pallas_call | solution.py:322
Async XLA Ops:
  0.6 85.0 %copy-start = (bf16[3584,1024]{1,0:T(8,128)(2,1)S(1)}, bf16[3584,1024]{1,0:T(8,128)(2,1)}, u32[]{:S(2)}) copy-start(bf16[3584,1024]{1,0:T(8,128)(2,1)} %probe.1) | copy-start | bytes 22020100
  0.6 1.3 %copy-start.1 = (bf16[3584,128]{1,0:T(8,128)(2,1)S(1)}, bf16[3584,128]{1,0:T(8,128)(2,1)}, u32[]{:S(2)}) copy-start(bf16[3584,128]{1,0:T(8,128)(2,1)} %hid_in.1) | copy-start | bytes 2752516
  2.0 1.1 %copy-start.2 = (bf16[64,1024]{1,0:T(8,128)(2,1)S(1)}, bf16[64,1024]{1,0:T(8,128)(2,1)}, u32[]{:S(2)}) copy-start(bf16[64,1024]{1,0:T(8,128)(2,1)} %target_in.1) | copy-start | bytes 393220
